TPU v7x, 32 devices: a whole 2x2x4 slice. The times are simulated.
32 devices in a mesh: dp: 8 (over z, y), mp: 4 (over x, core).
Axes of the slice: x: 2, y: 2, z: 4, core: 2. Of those that a mesh axis runs over, the one named last changes fastest.
Arguments:
- tokens: bfloat16 [8, 2048, 768], P('dp'), may hold values from -6 to 6
- cotangent: bfloat16 [8, 2048, 768], P('dp'), may hold values from -6 to 6
- capacity: int32 [8], replicated, may hold values from 256 to 1024, as said below
- selected: int32 [8, 1024], P('dp'), may hold values from 0 to 2047, as said below
- qkv_master: float32 [3, 768, 768], P(None, 'dp', 'mp'), may hold values from -0.21875 to 0.21875
- out_master: float32 [768, 768], P('mp', 'dp'), may hold values from -0.75 to 0.75
- up_master: float32 [768, 3072], P('dp', 'mp'), may hold values from -0.21875 to 0.21875
- down_master: float32 [3072, 768], P('mp', 'dp'), may hold values from -0.109375 to 0.109375
- vec_master: float32 [3, 768], P(None, 'dp')
- qkv_first: float32 [3, 768, 768], P(None, 'dp', 'mp'), may hold values from -48 to 48
- out_first: float32 [768, 768], P('mp', 'dp'), may hold values from -6 to 6
- up_first: float32 [768, 3072], P('dp', 'mp'), may hold values from -6 to 6
- down_first: float32 [3072, 768], P('mp', 'dp'), may hold values from -16 to 16
- vec_first: float32 [3, 768], P(None, 'dp')
- qkv_second: float32 [3, 768, 768], P(None, 'dp', 'mp'), may hold values from 127.7952 to 2064.384
- out_second: float32 [768, 768], P('mp', 'dp'), may hold values from 5.111808 to 82.57536
- up_second: float32 [768, 3072], P('dp', 'mp'), may hold values from 1.8402508 to 29.727129
- down_second: float32 [3072, 768], P('mp', 'dp'), may hold values from 14.057472 to 227.08224
- vec_second: float32 [3, 768], P(None, 'dp')
Outputs:
- block_out: bfloat16 [8, 2048, 768], P('dp')
- input_grad: float32 [8, 2048, 768], P('dp')
- qkv_new: float32 [3, 768, 768], P(None, 'dp', 'mp')
- out_new: float32 [768, 768], P('mp', 'dp')
- up_new: float32 [768, 3072], P('dp', 'mp')
- down_new: float32 [3072, 768], P('mp', 'dp')
- vec_new: float32 [3, 768], P(None, 'dp')
- qkv_first_new: float32 [3, 768, 768], P(None, 'dp', 'mp')
- out_first_new: float32 [768, 768], P('mp', 'dp')
- up_first_new: float32 [768, 3072], P('dp', 'mp')
- down_first_new: float32 [3072, 768], P('mp', 'dp')
- vec_first_new: float32 [3, 768], P(None, 'dp')
- qkv_second_new: float32 [3, 768, 768], P(None, 'dp', 'mp')
- out_second_new: float32 [768, 768], P('mp', 'dp')
- up_second_new: float32 [768, 3072], P('dp', 'mp')
- down_second_new: float32 [3072, 768], P('mp', 'dp')
- vec_second_new: float32 [3, 768], P(None, 'dp')
Inputs may be any that keep to these rules, and one draw needn't show every extreme that they name: Every sequence's capacity is 1024, 512 or 256; the sequences come in 4 batches of consecutive sequences that share one capacity, and each of the three values is used by some batch. Each row holds distinct positions: its first capacity[s] entries are the selected positions in ascending order, the rest are other positions in ascending order.
All inputs are finite; a program needn't handle non-finite values.
Results may differ from a plain program's by a relative error of at most 0.012.
Values may be sent and summed in bfloat16 or wider, within the bound.
A program may use at most 128 MiB of HBM per device.

v0:
```python
import jax
import jax.numpy as jnp
from jax import lax
from jax.sharding import PartitionSpec as P

MODEL_DIM = 768
HEAD_DIM = 64
STEP = 10


NORM_EPS = 1e-05
MASKED_SCORE = -1000000000.0
MOMENT_DECAY = 0.9
SQUARE_DECAY = 0.95
ADAM_EPS = 1e-08
WEIGHT_DECAY = 0.1
RATE_MATRIX = 0.06
RATE_VECTOR = 0.2


def gelu_tanh(values):
    return (
        0.5
        * values
        * (1.0 + jnp.tanh(0.7978845608028654 * (values + 0.044715 * values * values * values)))
    )


def scaled_norm(values, gain_row):
    inverse = lax.rsqrt(jnp.mean(values * values, axis=-1, keepdims=True) + NORM_EPS)
    normed = values * inverse
    return (normed, inverse, normed * gain_row)


def contract_rows(left_side, right_side):
    return lax.dot_general(
        left_side, right_side, (((0,), (0,)), ((), ())), preferred_element_type=jnp.float32
    )


def contract_cols(left_side, right_side):
    return lax.dot_general(
        left_side, right_side, (((1,), (1,)), ((), ())), preferred_element_type=jnp.float32
    )


def live_blocks(count, row_count, block_fn, init):
    block_rows = min(256, row_count)
    trip_count = (count + block_rows - 1) // block_rows

    def run_block(number, carry_state):
        return block_fn(number * block_rows, block_rows, carry_state)

    return lax.fori_loop(0, trip_count, run_block, init)


def first_rows(row_low, count, gain_row, w_qkv):
    row_count = row_low.shape[0]
    normed, inverse, scaled = scaled_norm(row_low.astype(jnp.float32), gain_row)
    normed_low = scaled.astype(jnp.bfloat16)

    def project(offset, block_rows, result):
        part = lax.dynamic_slice_in_dim(normed_low, offset, block_rows, 0)
        value = jnp.einsum("cd,tde->tce", part, w_qkv, preferred_element_type=jnp.float32).astype(
            jnp.bfloat16
        )
        return lax.dynamic_update_slice_in_dim(result, value, offset, 1)

    start = jnp.zeros((3, row_count, w_qkv.shape[2]), jnp.bfloat16)
    return (live_blocks(count, row_count, project, start), normed_low, normed, inverse)


def tile_scores(query_block, key_block, query_start, key_start, count):
    scores = jnp.einsum(
        "qhd,khd->hqk", query_block, key_block, preferred_element_type=jnp.float32
    ) * HEAD_DIM ** (-0.5)
    query_pos = query_start + jnp.arange(query_block.shape[0], dtype=jnp.int32)
    key_pos = key_start + jnp.arange(key_block.shape[0], dtype=jnp.int32)
    allowed = (key_pos[None, :] <= query_pos[:, None]) & (key_pos[None, :] < count)
    return jnp.where(allowed[None], scores, MASKED_SCORE)


def attend(qkv_rows, count):
    row_count = qkv_rows.shape[1]
    local_heads = qkv_rows.shape[2] // HEAD_DIM
    heads = qkv_rows.reshape(3, row_count, local_heads, HEAD_DIM)
    block_rows = min(512, row_count)
    trip_count = (count + block_rows - 1) // block_rows

    def one_query(number, carry_state):
        mixed, log_sums = carry_state
        query_start = number * block_rows
        query_block = lax.dynamic_slice_in_dim(heads[0], query_start, block_rows, 0)

        def statistics(key_number, stats):
            running_max, running_sum = stats
            key_start = key_number * block_rows
            key_block = lax.dynamic_slice_in_dim(heads[1], key_start, block_rows, 0)
            scores = tile_scores(query_block, key_block, query_start, key_start, count)
            new_max = jnp.maximum(running_max, jnp.max(scores, axis=-1))
            new_sum = running_sum * jnp.exp(running_max - new_max) + jnp.sum(
                jnp.exp(scores - new_max[..., None]), axis=-1
            )
            return (new_max, new_sum)

        start_stats = (
            jnp.full((local_heads, block_rows), -1e30, jnp.float32),
            jnp.zeros((local_heads, block_rows), jnp.float32),
        )
        row_max, row_sum = lax.fori_loop(0, number + 1, statistics, start_stats)
        row_lse = row_max + jnp.log(row_sum)

        def accumulate(key_number, total):
            key_start = key_number * block_rows
            key_block = lax.dynamic_slice_in_dim(heads[1], key_start, block_rows, 0)
            value_block = lax.dynamic_slice_in_dim(heads[2], key_start, block_rows, 0)
            probs = jnp.exp(
                tile_scores(query_block, key_block, query_start, key_start, count)
                - row_lse[..., None]
            )
            return total + jnp.einsum(
                "hqk,khd->qhd",
                probs.astype(jnp.bfloat16),
                value_block,
                preferred_element_type=jnp.float32,
            )

        result = lax.fori_loop(
            0, number + 1, accumulate, jnp.zeros((block_rows, local_heads, HEAD_DIM), jnp.float32)
        )
        mixed = lax.dynamic_update_slice_in_dim(
            mixed,
            result.reshape(block_rows, local_heads * HEAD_DIM).astype(jnp.bfloat16),
            query_start,
            0,
        )
        log_sums = lax.dynamic_update_slice_in_dim(log_sums, row_lse, query_start, 1)
        return (mixed, log_sums)

    start = (
        jnp.zeros((row_count, local_heads * HEAD_DIM), jnp.bfloat16),
        jnp.zeros((local_heads, row_count), jnp.float32),
    )
    return lax.fori_loop(0, trip_count, one_query, start)


def attend_back(qkv_rows, log_sums, mixed_grad, count):
    row_count = qkv_rows.shape[1]
    local_heads = qkv_rows.shape[2] // HEAD_DIM
    heads = qkv_rows.reshape(3, row_count, local_heads, HEAD_DIM)
    grad_heads = mixed_grad.reshape(row_count, local_heads, HEAD_DIM)
    block_rows = min(512, row_count)
    trip_count = (count + block_rows - 1) // block_rows
    scale = HEAD_DIM ** (-0.5)

    def one_query(number, carry_state):
        query_total, key_total, value_total = carry_state
        query_start = number * block_rows
        query_block = lax.dynamic_slice_in_dim(heads[0], query_start, block_rows, 0)
        grad_block = lax.dynamic_slice_in_dim(grad_heads, query_start, block_rows, 0)
        row_lse = lax.dynamic_slice_in_dim(log_sums, query_start, block_rows, 1)

        def tile_terms(key_number):
            key_start = key_number * block_rows
            key_block = lax.dynamic_slice_in_dim(heads[1], key_start, block_rows, 0)
            value_block = lax.dynamic_slice_in_dim(heads[2], key_start, block_rows, 0)
            probs = jnp.exp(
                tile_scores(query_block, key_block, query_start, key_start, count)
                - row_lse[..., None]
            )
            prob_grad = jnp.einsum(
                "qhd,khd->hqk", grad_block, value_block, preferred_element_type=jnp.float32
            )
            return (key_start, key_block, probs, prob_grad)

        def row_dots(key_number, total):
            terms = tile_terms(key_number)
            return total + jnp.sum(terms[2] * terms[3], axis=-1)

        dots = lax.fori_loop(
            0, number + 1, row_dots, jnp.zeros((local_heads, block_rows), jnp.float32)
        )

        def gradients(key_number, inner_state):
            query_acc, key_acc, value_acc = inner_state
            key_start, key_block, probs, prob_grad = tile_terms(key_number)
            score_grad = (probs * (prob_grad - dots[..., None])).astype(jnp.bfloat16)
            query_acc = (
                query_acc
                + jnp.einsum(
                    "hqk,khd->qhd", score_grad, key_block, preferred_element_type=jnp.float32
                )
                * scale
            )
            key_part = (
                jnp.einsum(
                    "hqk,qhd->khd", score_grad, query_block, preferred_element_type=jnp.float32
                )
                * scale
            )
            value_part = jnp.einsum(
                "hqk,qhd->khd",
                probs.astype(jnp.bfloat16),
                grad_block,
                preferred_element_type=jnp.float32,
            )
            key_acc = lax.dynamic_update_slice_in_dim(
                key_acc,
                lax.dynamic_slice_in_dim(key_acc, key_start, block_rows, 0) + key_part,
                key_start,
                0,
            )
            value_acc = lax.dynamic_update_slice_in_dim(
                value_acc,
                lax.dynamic_slice_in_dim(value_acc, key_start, block_rows, 0) + value_part,
                key_start,
                0,
            )
            return (query_acc, key_acc, value_acc)

        start_inner = (
            jnp.zeros((block_rows, local_heads, HEAD_DIM), jnp.float32),
            key_total,
            value_total,
        )
        query_acc, key_total, value_total = lax.fori_loop(0, number + 1, gradients, start_inner)
        query_total = lax.dynamic_update_slice_in_dim(query_total, query_acc, query_start, 0)
        return (query_total, key_total, value_total)

    empty = jnp.zeros((row_count, local_heads, HEAD_DIM), jnp.float32)
    query_total, key_total, value_total = lax.fori_loop(
        0, trip_count, one_query, (empty, empty, empty)
    )
    return (
        jnp.stack([query_total, key_total, value_total])
        .astype(jnp.bfloat16)
        .reshape(3, row_count, local_heads * HEAD_DIM)
    )


def feed_forward(row_data, live_rows, gain_row, w_up, w_down):
    row_count = row_data.shape[0]
    block_rows = min(128, row_count)
    normed_low = scaled_norm(row_data.astype(jnp.float32), gain_row)[2].astype(jnp.bfloat16)

    def run_block(number, result):
        offset = number * block_rows
        row_block = lax.dynamic_slice_in_dim(normed_low, offset, block_rows, 0)
        up_proj = jnp.dot(row_block, w_up, preferred_element_type=jnp.float32)
        activated = gelu_tanh(up_proj).astype(jnp.bfloat16)
        return lax.dynamic_update_slice_in_dim(
            result, jnp.dot(activated, w_down, preferred_element_type=jnp.float32), offset, 0
        )

    trip_count = (live_rows + block_rows - 1) // block_rows
    partial_rows = lax.fori_loop(
        0, trip_count, run_block, jnp.zeros((row_count, w_down.shape[1]), jnp.float32)
    )
    return lax.psum(partial_rows.astype(jnp.bfloat16), "mp").astype(jnp.float32)


def feed_back(row_data, grad_rows, live_rows, gain_row, w_up, w_down):
    row_count = row_data.shape[0]
    block_rows = min(128, row_count)
    normed, inverse, scaled = scaled_norm(row_data.astype(jnp.float32), gain_row)
    normed_low = scaled.astype(jnp.bfloat16)

    def run_block(number, carry_state):
        input_part, up_grad, down_grad = carry_state
        offset = number * block_rows
        row_block = lax.dynamic_slice_in_dim(normed_low, offset, block_rows, 0)
        grad_block = lax.dynamic_slice_in_dim(grad_rows, offset, block_rows, 0)
        up_proj = jnp.dot(row_block, w_up, preferred_element_type=jnp.float32)
        activated, gelu_pull = jax.vjp(gelu_tanh, up_proj)
        down_grad = down_grad + contract_rows(activated.astype(jnp.bfloat16), grad_block)
        act_grad = contract_cols(grad_block, w_down)
        up_low = gelu_pull(act_grad)[0].astype(jnp.bfloat16)
        up_grad = up_grad + contract_rows(row_block, up_low)
        input_part = lax.dynamic_update_slice_in_dim(
            input_part, contract_cols(up_low, w_up), offset, 0
        )
        return (input_part, up_grad, down_grad)

    trip_count = (live_rows + block_rows - 1) // block_rows
    start_state = (
        jnp.zeros((row_count, w_up.shape[0]), jnp.float32),
        jnp.zeros(w_up.shape, jnp.float32),
        jnp.zeros(w_down.shape, jnp.float32),
    )
    input_part, up_grad, down_grad = lax.fori_loop(0, trip_count, run_block, start_state)
    normed_grad = lax.psum(input_part, "mp")
    gain_grad = jnp.sum(normed_grad * normed, axis=0)
    scaled_grad = normed_grad * gain_row
    row_grad = inverse * (
        scaled_grad - normed * jnp.mean(scaled_grad * normed, axis=-1, keepdims=True)
    )
    return (row_grad.astype(jnp.bfloat16), up_grad, down_grad, gain_grad)


def second_rows(row_low, mixed, count, vectors, gain_rows, w_out, w_up, w_down):
    row_count = row_low.shape[0]
    rows_full = row_low.astype(jnp.float32)

    def apply_out(offset, block_rows, result):
        part = lax.dynamic_slice_in_dim(mixed, offset, block_rows, 0)
        return lax.dynamic_update_slice_in_dim(
            result, jnp.dot(part, w_out, preferred_element_type=jnp.float32), offset, 0
        )

    partial_rows = live_blocks(
        count, row_count, apply_out, jnp.zeros((row_count, w_out.shape[1]), jnp.float32)
    )
    attended = lax.psum(partial_rows, "mp")
    summed_low = (rows_full + attended).astype(jnp.bfloat16)
    branch_full = (
        feed_forward(summed_low, count, gain_rows[1], w_up, w_down)
        .astype(jnp.bfloat16)
        .astype(jnp.float32)
    )
    gate_value = jax.nn.sigmoid(
        jnp.dot(row_low, vectors[2], preferred_element_type=jnp.float32) * MODEL_DIM ** (-0.5)
    )
    updated = rows_full + gate_value[:, None] * (attended + branch_full)
    return (updated.astype(jnp.bfloat16), attended, branch_full, gate_value, summed_low)


def second_back(
    out_grad,
    mixed,
    summed_low,
    attended,
    branch_full,
    gate_value,
    count,
    gain_rows,
    w_out,
    w_up,
    w_down,
):
    row_count = out_grad.shape[0]
    branch_grad = out_grad * gate_value[:, None]
    gate_grad = jnp.sum(out_grad * (attended + branch_full), axis=-1)
    logit_grad = gate_grad * gate_value * (1.0 - gate_value) * MODEL_DIM ** (-0.5)
    summed_grad, up_grad, down_grad, second_gain = feed_back(
        summed_low, branch_grad.astype(jnp.bfloat16), count, gain_rows[1], w_up, w_down
    )
    summed_full = summed_grad.astype(jnp.float32)
    attn_grad = (branch_grad + summed_full).astype(jnp.bfloat16)

    def out_block(offset, block_rows, carry_state):
        weight_grad, mixed_grad = carry_state
        grad_part = lax.dynamic_slice_in_dim(attn_grad, offset, block_rows, 0)
        mixed_part = lax.dynamic_slice_in_dim(mixed, offset, block_rows, 0)
        weight_grad = weight_grad + contract_rows(mixed_part, grad_part)
        value = contract_cols(grad_part, w_out).astype(jnp.bfloat16)
        return (weight_grad, lax.dynamic_update_slice_in_dim(mixed_grad, value, offset, 0))

    start = (
        jnp.zeros(w_out.shape, jnp.float32),
        jnp.zeros((row_count, w_out.shape[0]), jnp.bfloat16),
    )
    out_wgrad, mixed_grad = live_blocks(count, row_count, out_block, start)
    return (mixed_grad, out_wgrad, up_grad, down_grad, second_gain, summed_full, logit_grad)


def first_back(proj_grad, normed_low, normed, inverse, count, gain_row, w_qkv):
    row_count = normed_low.shape[0]

    def qkv_block(offset, block_rows, carry_state):
        weight_grad, input_part = carry_state
        grad_part = lax.dynamic_slice_in_dim(proj_grad, offset, block_rows, 1)
        row_part = lax.dynamic_slice_in_dim(normed_low, offset, block_rows, 0)
        weight_grad = weight_grad + jnp.einsum(
            "cd,tce->tde", row_part, grad_part, preferred_element_type=jnp.float32
        )
        value = jnp.einsum("tce,tde->cd", grad_part, w_qkv, preferred_element_type=jnp.float32)
        return (weight_grad, lax.dynamic_update_slice_in_dim(input_part, value, offset, 0))

    start = (
        jnp.zeros(w_qkv.shape, jnp.float32),
        jnp.zeros((row_count, w_qkv.shape[1]), jnp.float32),
    )
    qkv_wgrad, input_part = live_blocks(count, row_count, qkv_block, start)
    first_grad = lax.psum(input_part.astype(jnp.bfloat16), "mp").astype(jnp.float32)
    first_gain = jnp.sum(first_grad * normed, axis=0)
    scaled_grad = first_grad * gain_row
    norm_grad = inverse * (
        scaled_grad - normed * jnp.mean(scaled_grad * normed, axis=-1, keepdims=True)
    )
    return (norm_grad, qkv_wgrad, first_gain)


def adam_update(master, first_moment, second_moment, gradient, step_rate, decay_rate):
    first_new = MOMENT_DECAY * first_moment + (1.0 - MOMENT_DECAY) * gradient
    second_new = SQUARE_DECAY * second_moment + (1.0 - SQUARE_DECAY) * gradient * gradient
    first_hat = first_new / (1.0 - MOMENT_DECAY**STEP)
    second_hat = second_new / (1.0 - SQUARE_DECAY**STEP)
    master_new = master - step_rate * (
        first_hat / (jnp.sqrt(second_hat) + ADAM_EPS) + decay_rate * master
    )
    return (master_new, first_new, second_new)


def local(
    tokens,
    cotangent,
    capacity,
    selected,
    qkv_master,
    out_master,
    up_master,
    down_master,
    vec_master,
    qkv_first,
    out_first,
    up_first,
    down_first,
    vec_first,
    qkv_second,
    out_second,
    up_second,
    down_second,
    vec_second,
):
    low_type = jnp.bfloat16
    w_qkv, w_out, w_up, w_down, vectors = (
        lax.all_gather(qkv_master.astype(low_type), "dp", axis=1, tiled=True),
        lax.all_gather(out_master.astype(low_type), "dp", axis=1, tiled=True),
        lax.all_gather(up_master.astype(low_type), "dp", axis=0, tiled=True),
        lax.all_gather(down_master.astype(low_type), "dp", axis=1, tiled=True),
        lax.all_gather(vec_master.astype(low_type), "dp", axis=1, tiled=True),
    )
    gain_rows = vectors.astype(jnp.float32)
    seq_len = tokens.shape[1]
    model_width = tokens.shape[2]
    chosen = selected[0]
    slot_count = chosen.shape[0]
    local_width = w_qkv.shape[2]
    device = lax.axis_index("dp")
    groups = lax.axis_size("dp")
    spread = slot_count // groups
    own_count = capacity[device]
    slot_ids = jnp.arange(slot_count, dtype=jnp.int32)
    live_mask = slot_ids < own_count
    target = jnp.where(live_mask, chosen, seq_len)
    one_sequence = tokens[0]
    rows_low = one_sequence[chosen]
    flat_ids = jnp.arange(slot_count, dtype=jnp.int32)
    source = flat_ids % groups
    home_slot = flat_ids // groups * groups + device
    held_mask = home_slot < capacity[source]
    row_order = jnp.argsort(jnp.where(held_mask, flat_ids, flat_ids + slot_count), stable=True)
    restore = jnp.argsort(row_order, stable=True)
    held_count = jnp.sum(held_mask.astype(jnp.int32))
    work_rows = lax.all_to_all(
        rows_low.reshape(spread, groups, model_width), "dp", split_axis=1, concat_axis=1, tiled=True
    ).reshape(slot_count, model_width)[row_order]
    projected, normed_low, normed_one, inverse_one = first_rows(
        work_rows, held_count, gain_rows[0], w_qkv
    )
    qkv_home = lax.all_to_all(
        projected[:, restore].reshape(3, spread, groups, local_width),
        "dp",
        split_axis=2,
        concat_axis=2,
        tiled=True,
    ).reshape(3, slot_count, local_width)
    mixed_home, log_sums = attend(qkv_home, own_count)
    mixed_rows = lax.all_to_all(
        mixed_home.reshape(spread, groups, local_width),
        "dp",
        split_axis=1,
        concat_axis=1,
        tiled=True,
    ).reshape(slot_count, local_width)[row_order]
    updated_low, attended, branch_full, gate_value, summed_low = second_rows(
        work_rows, mixed_rows, held_count, vectors, gain_rows, w_out, w_up, w_down
    )
    updated_home = lax.all_to_all(
        updated_low[restore].reshape(spread, groups, model_width),
        "dp",
        split_axis=1,
        concat_axis=1,
        tiled=True,
    ).reshape(slot_count, model_width)
    block_out = one_sequence.at[target].set(updated_home, mode="drop")[None]
    cot_low = cotangent[0]
    out_low = jnp.where(live_mask[:, None], cot_low[chosen], jnp.zeros((), low_type))
    out_rows = lax.all_to_all(
        out_low.reshape(spread, groups, model_width), "dp", split_axis=1, concat_axis=1, tiled=True
    ).reshape(slot_count, model_width)[row_order]
    out_grad = out_rows.astype(jnp.float32)
    mixed_grad, out_wgrad, up_grad, down_grad, second_gain, summed_full, logit_grad = second_back(
        out_grad,
        mixed_rows,
        summed_low,
        attended,
        branch_full,
        gate_value,
        held_count,
        gain_rows,
        w_out,
        w_up,
        w_down,
    )
    mixed_grad_home = lax.all_to_all(
        mixed_grad[restore].reshape(spread, groups, local_width),
        "dp",
        split_axis=1,
        concat_axis=1,
        tiled=True,
    ).reshape(slot_count, local_width)
    proj_grad_home = attend_back(qkv_home, log_sums, mixed_grad_home, own_count)
    proj_grad = lax.all_to_all(
        proj_grad_home.reshape(3, spread, groups, local_width),
        "dp",
        split_axis=2,
        concat_axis=2,
        tiled=True,
    ).reshape(3, slot_count, local_width)[:, row_order]
    norm_grad, qkv_wgrad, first_gain = first_back(
        proj_grad, normed_low, normed_one, inverse_one, held_count, gain_rows[0], w_qkv
    )
    rows_full = work_rows.astype(jnp.float32)
    rows_grad = out_grad + summed_full + norm_grad + logit_grad[:, None] * gain_rows[2][None, :]
    router_grad = jnp.dot(logit_grad, rows_full, precision=lax.Precision.HIGHEST)
    rows_grad_home = (
        lax.all_to_all(
            rows_grad[restore].reshape(spread, groups, model_width).astype(jnp.bfloat16),
            "dp",
            split_axis=1,
            concat_axis=1,
            tiled=True,
        )
        .astype(jnp.float32)
        .reshape(slot_count, model_width)
    )
    input_grad = cot_low.astype(jnp.float32).at[target].set(rows_grad_home, mode="drop")[None]
    vector_grad = jnp.stack([first_gain, second_gain, router_grad])
    qkv_sum, out_sum, up_sum, down_sum, vec_sum = (
        lax.psum_scatter(qkv_wgrad, "dp", scatter_dimension=1, tiled=True),
        lax.psum_scatter(out_wgrad, "dp", scatter_dimension=1, tiled=True),
        lax.psum_scatter(up_grad, "dp", scatter_dimension=0, tiled=True),
        lax.psum_scatter(down_grad, "dp", scatter_dimension=1, tiled=True),
        lax.psum_scatter(vector_grad, "dp", scatter_dimension=1, tiled=True),
    )
    qkv_res = adam_update(qkv_master, qkv_first, qkv_second, qkv_sum, RATE_MATRIX, WEIGHT_DECAY)
    out_res = adam_update(out_master, out_first, out_second, out_sum, RATE_MATRIX, WEIGHT_DECAY)
    up_res = adam_update(up_master, up_first, up_second, up_sum, RATE_MATRIX, WEIGHT_DECAY)
    down_res = adam_update(
        down_master, down_first, down_second, down_sum, RATE_MATRIX, WEIGHT_DECAY
    )
    vec_res = adam_update(vec_master, vec_first, vec_second, vec_sum, RATE_VECTOR, 0.0)
    return (
        block_out,
        input_grad,
        qkv_res[0],
        out_res[0],
        up_res[0],
        down_res[0],
        vec_res[0],
        qkv_res[1],
        out_res[1],
        up_res[1],
        down_res[1],
        vec_res[1],
        qkv_res[2],
        out_res[2],
        up_res[2],
        down_res[2],
        vec_res[2],
    )


def solution(mesh):
    return jax.shard_map(
        local,
        mesh=mesh,
        in_specs=(
            P("dp", None, None),
            P("dp", None, None),
            P(),
            P("dp", None),
            P(None, "dp", "mp"),
            P("mp", "dp"),
            P("dp", "mp"),
            P("mp", "dp"),
            P(None, "dp"),
            P(None, "dp", "mp"),
            P("mp", "dp"),
            P("dp", "mp"),
            P("mp", "dp"),
            P(None, "dp"),
            P(None, "dp", "mp"),
            P("mp", "dp"),
            P("dp", "mp"),
            P("mp", "dp"),
            P(None, "dp"),
        ),
        out_specs=(
            P("dp", None, None),
            P("dp", None, None),
            P(None, "dp", "mp"),
            P("mp", "dp"),
            P("dp", "mp"),
            P("mp", "dp"),
            P(None, "dp"),
            P(None, "dp", "mp"),
            P("mp", "dp"),
            P("dp", "mp"),
            P("mp", "dp"),
            P(None, "dp"),
            P(None, "dp", "mp"),
            P("mp", "dp"),
            P("dp", "mp"),
            P("mp", "dp"),
            P(None, "dp"),
        ),
        check_vma=False,
    )
```

profile of v0, /device:TPU:0, one launch (start us, length us, event | category | flops | bytes accessed | tf_op | source)
XLA Modules:
  0.0 1052.0 jit_solution(11108735352390810278)
XLA Ops:
  20.0 7.4 all-to-all-start
  34.0 34.3 %all-gather = bf16[8,96,3]{1,2,0:T(4,128)(2,1)S(1)} all-gather(bf16[1,96,3]{1,2,0:T(4,128)(2,1)S(1)} %convert_bitcast_fusion.1), channel_id=1, replica_groups=mesh['dp'=8,'mp'=4] {'dp'}, dimensions={0}, use_global_device_ids=true | all-gather | bytes 5184 | tf_op jit(solution)/shard_map/all_gather | solution.py:431
  68.5 40.5 %all_gather.16 = bf16[3,768,192]{2,0,1:T(4,128)(2,1)S(1)} all-gather(bf16[3,96,192]{2,0,1:T(4,128)(2,1)S(1)} %copy.120), channel_id=1, replica_groups=mesh['dp'=8,'mp'=4] {'dp'}, dimensions={1}, use_global_device_ids=true | all-gather | bytes 995328 | tf_op jit(solution)/shard_map/all_gather | solution.py:427
  138.4 10.1 gather_fusion.2
  158.9 27.3 %all-to-all-done.1 = bf16[3,128,8,192]{1,3,0,2:T(8,128)(2,1)S(1)} async-done(((bf16[3,128,8,192]{1,3,0,2:T(8,128)(2,1)}), bf16[3,128,8,192]{1,3,0,2:T(8,128)(2,1)S(1)}, u32[]{:S(2)}, u32[]{:S(2)}) %all-to-all-start.1) | async-done | bytes 1179680 | tf_op jit(solution)/shard_map/all_to_all | solution.py:461
  194.7 15.2 %while.143 = (s32[]{:T(128)}, bf16[1024,192]{0,1:T(8,128)(2,1)S(1)}, f32[3,1024]{1,0:T(4,128)S(1)}, s32[]{:T(128)}, bf16[3,1024,3,64]{1,3,2,0:T(8,128)(2,1)S(1)}...) while((s32[]{:T(128)}, bf16[1024,192]{0,1:T(8,128)(2,1)S(1)}, ...), condition=%wide.region_13.14_spmd, body=%wide.region_6.13_spmd.sunk | while | flops 311894528 | bytes 14440245 | solution.py:144
  214.8 33.8 %all_gather.17 = bf16[192,768]{0,1:T(8,128)(2,1)S(1)} all-gather(bf16[192,96]{0,1:T(8,128)(2,1)S(1)} %copy.130), channel_id=1, replica_groups=mesh['dp'=8,'mp'=4] {'dp'}, dimensions={1}, use_global_device_ids=true | all-gather | bytes 331776 | tf_op jit(solution)/shard_map/all_gather | solution.py:428
  248.7 6.8 gather_fusion.5
  276.9 11.3 %all-to-all-done.4 = bf16[128,8,768]{2,0,1:T(8,128)(2,1)} async-done(((bf16[128,8,768]{2,0,1:T(8,128)(2,1)}), bf16[128,8,768]{2,0,1:T(8,128)(2,1)}, u32[]{:S(2)}, u32[]{:S(2)}) %all-to-all-start.4) | async-done | bytes 1572896 | tf_op jit(solution)/shard_map/all_to_all | solution.py:489
  297.9 43.8 %all-reduce.5.cloned.1.call-done = f32[1024,768]{1,0:T(8,128)} async-done(((f32[1024,768]{1,0:T(8,128)}), f32[1024,768]{1,0:T(8,128)}) %all-reduce.5.cloned.1.call-update) | async-done | bytes 3145744 | tf_op jit(solution)/shard_map/psum | solution.py:313
  352.7 72.4 %while.146 = (s32[]{:T(128)}, f32[1024,768]{1,0:T(8,128)}, f32[768,768]{1,0:T(8,128)}, f32[768,768]{1,0:T(8,128)}, s32[]{:T(128)}, /*index=5*/bf16[1024,768]{1,0...) while((s32[]{:T(128)}, f32[1024,768]{1,0:T(8,128)}, ...), condition=%wide.region_23.24_spmd, body=%wide.region_22.23_spmd.sunk | while | flops 759398400 | bytes 15925439 | solution.py:290
  425.1 68.4 %all-reduce.7.cloned.1.call-done = f32[1024,768]{1,0:T(8,128)} async-done(((f32[1024,768]{1,0:T(8,128)}), f32[1024,768]{1,0:T(8,128)}) %all-reduce.7.cloned.1.call-update) | async-done | bytes 3145744 | tf_op jit(solution)/shard_map/psum | solution.py:291
  501.6 8.2 while.147
  515.9 5.5 all-to-all-start.5
  521.5 11.5 %all-to-all-done.5 = bf16[128,8,192]{0,2,1:T(8,128)(2,1)S(1)} async-done(((bf16[128,8,192]{0,2,1:T(8,128)(2,1)}), bf16[128,8,192]{0,2,1:T(8,128)(2,1)S(1)}, u32[]{:S(2)}, u32[]{:S(2)}) %all-to-all-start.5) | async-done | bytes 393248 | tf_op jit(solution)/shard_map/all_to_all | solution.py:506
  535.3 30.0 %while.150 = (s32[]{:T(128)}, bf16[1024,3,64]{0,2,1:T(8,128)(2,1)S(1)}, f32[1024,3,64]{0,2,1:T(8,128)S(1)}, f32[1024,3,64]{0,2,1:T(8,128)}, s32[]{:T(128)}, /*in...) while((s32[]{:T(128)}, ...), condition=%wide.region_34.35_spmd, body=%wide.region_28.34_spmd.sunk | while | flops 717983744 | bytes 32271276 | solution.py:231
  539.0 6.6 while.155
  546.5 5.7 while.154
  552.2 13.2 %while.155 = (s32[]{:T(128)}, f32[512,3,64]{0,2,1:T(8,128)S(1)}, f32[1024,3,64]{0,2,1:T(8,128)S(1)}, f32[1024,3,64]{0,2,1:T(8,128)}, s32[]{:T(128)}, /*index=5*/...) while((s32[]{:T(128)}, f32[512,3,64]{0,2,1:T(8,128)S(1)}, ...), condition=%wide.region_33.33_spmd, body=%wide.region_32.32_spmd.sunk | while | flops 512198656 | bytes 20282600 | solution.py:226
  579.1 12.4 %while.145 = (s32[]{:T(128)}, bf16[1024,768]{1,0:T(8,128)(2,1)S(1)}, s32[]{:T(128)}, bf16[1024,768]{1,0:T(8,128)(2,1)}, bf16[768,768]{1,0:T(8,128)(2,1)S(1)}, /*...) while((s32[]{:T(128)}, bf16[1024,768]{1,0:T(8,128)(2,1)S(1)}, s32[]{:T(128)}, ...), condition=%wide.region_19.20_spmd, body=%wide.region_18.19_spmd.sunk | while | flops 302874624 | bytes 2950291 | solution.py:256
  591.6 11.6 %all-to-all-done.6 = bf16[3,128,8,192]{1,3,0,2:T(8,128)(2,1)} async-done(((bf16[3,128,8,192]{1,3,0,2:T(8,128)(2,1)}), bf16[3,128,8,192]{1,3,0,2:T(8,128)(2,1)}, u32[]{:S(2)}, u32[]{:S(2)}) %all-to-all-start.6) | async-done | bytes 1179680 | tf_op jit(solution)/shard_map/all_to_all | solution.py:514
  610.2 10.2 gather_fusion.8
  624.6 11.3 %while.151 = (s32[]{:T(128)}, f32[3,768,192]{1,2,0:T(8,128)S(1)}, bf16[1024,768]{1,0:T(8,128)(2,1)}, s32[]{:T(128)}, bf16[3,1024,192]{1,2,0:T(8,128)(2,1)}, /*in...) while((s32[]{:T(128)}, f32[3,768,192]{1,2,0:T(8,128)S(1)}, ...), condition=%wide.region_36.37_spmd, body=%wide.region_35.36_spmd.sunk | while | flops 453427200 | bytes 6195355 | solution.py:54
  642.6 60.4 %all-reduce.9.cloned.1.call-done = (bf16[1024,768]{1,0:T(8,128)(2,1)}, bf16[1024,768]{1,0:T(8,128)(2,1)}) async-done(((bf16[1024,768]{1,0:T(8,128)(2,1)}, bf16[1024,768]{1,0:T(8,128)(2,1)}), (bf16[1024,768]{1,0:T(8,128)(2,1)}, bf16[1024,768]{1,0:T(8,128)(2,1)})) %all-reduce.9.cloned.1.call-update) | async-done | bytes 3145744 | tf_op jit(solution)/shard_map/psum | solution.py:259
  717.9 5.7 all-to-all-start.7
  733.9 34.6 %all-to-all-done.7 = bf16[128,8,768]{2,0,1:T(8,128)(2,1)} async-done(((bf16[128,8,768]{2,0,1:T(8,128)(2,1)}), bf16[128,8,768]{2,0,1:T(8,128)(2,1)}, u32[]{:S(2)}, u32[]{:S(2)}) %all-to-all-start.7) | async-done | bytes 1572896 | tf_op jit(solution)/shard_map/all_to_all | solution.py:528
  779.1 19.6 %reduce-scatter.14.cloned.1.call-done = f32[768,96]{0,1:T(8,128)} async-done(((f32[768,768]{0,1:T(8,128)}), f32[768,96]{0,1:T(8,128)}) %reduce-scatter.14.cloned.1.call-update) | async-done | bytes 294928 | tf_op jit(solution)/shard_map/reduce_scatter | solution.py:544
  800.9 78.1 %reduce-scatter.12.cloned.1.call-done = f32[96,768]{1,0:T(8,128)} async-done(((f32[768,768]{1,0:T(8,128)}), f32[96,768]{1,0:T(8,128)}) %reduce-scatter.12.cloned.1.call-update) | async-done | bytes 294928 | tf_op jit(solution)/shard_map/reduce_scatter | solution.py:543
  881.0 61.9 %reduce-scatter.18.cloned.1.call-done = f32[96,3]{1,0:T(8,128)} async-done(((f32[768,3]{1,0:T(8,128)}), f32[96,3]{1,0:T(8,128)}) %reduce-scatter.18.cloned.1.call-update) | async-done | bytes 1168
  944.5 70.4 %reduce-scatter.10.cloned.1.call-done = f32[3,96,192]{2,1,0:T(8,128)} async-done(((f32[3,768,192]{2,1,0:T(8,128)}), f32[3,96,192]{2,1,0:T(8,128)}) %reduce-scatter.10.cloned.1.call-update) | async-done | bytes 221200 | tf_op jit(solution)/shard_map/reduce_scatter | solution.py:541
  1020.2 13.7 %scatter_custom_fusion.1 = f32[2048,768]{1,0:T(8,128)} fusion(f32[2048,768]{1,0:T(8,128)} %bitcast_convert_fusion, s32[1024]{0:T(1024)} %bitcast.338, f32[128,8,768]{2,0,1:T(8,128)} %reshape.445), kind=kCustom, calls=%fused_computation.213 | custom fusion | bytes 9437184 | tf_op jit(solution)/shard_map/scatter | solution.py:538
  1033.9 8.5 scatter_custom_fusion
  (449 shorter events, 380.1 us)
Async XLA Ops:
  20.0 99.3 %all-to-all-start = ((bf16[128,8,768]{2,0,1:T(8,128)(2,1)}), bf16[128,8,768]{2,0,1:T(8,128)(2,1)}, u32[]{:S(2)}, u32[]{:S(2)}) async-start(bf16[128,8,768]{2,0,1:T(8,128)(2,1)} %copy.117), calls=%async_computation | async-start | bytes 3145728 | tf_op jit(solution)/shard_map/all_to_all | solution.py:455
  119.3 171.2 %copy-start.42 = (s32[1024]{0:T(1024)}, s32[1024]{0:T(1024)S(1)}, u32[]{:S(2)}) copy-start(s32[1024]{0:T(1024)S(1)} %fusion.173) | copy-start | bytes 12292
  152.8 33.4 %all-to-all-start.1 = ((bf16[3,128,8,192]{1,3,0,2:T(8,128)(2,1)}), bf16[3,128,8,192]{1,3,0,2:T(8,128)(2,1)S(1)}, u32[]{:S(2)}, u32[]{:S(2)}) async-start(bf16[3,128,8,192]{1,3,0,2:T(8,128)(2,1)} %copy.124), calls=%async_computation.1 | async-start | bytes 2359296 | tf_op jit(solution)/shard_map/all_to_all | solution.py:461
  157.4 117.1 %all-gather.6.cloned.1.call-start = ((), (), s32[]{:S(2)}) async-start(), calls=%async_computation.15 | async-start | bytes 1327104 | tf_op jit(solution)/shard_map/all_gather | solution.py:430
  211.2 46.7 %all-to-all-start.2 = ((bf16[128,8,192]{0,2,1:T(8,128)(2,1)}), bf16[128,8,192]{0,2,1:T(8,128)(2,1)S(1)}, u32[]{:S(2)}, u32[]{:S(2)}) async-start(bf16[128,8,192]{0,2,1:T(8,128)(2,1)} %copy.128), calls=%async_computation.2 | async-start | bytes 786432 | tf_op jit(solution)/shard_map/all_to_all | solution.py:469
  258.0 30.3 %all-to-all-start.4 = ((bf16[128,8,768]{2,0,1:T(8,128)(2,1)}), bf16[128,8,768]{2,0,1:T(8,128)(2,1)}, u32[]{:S(2)}, u32[]{:S(2)}) async-start(bf16[128,8,768]{2,0,1:T(8,128)(2,1)} %copy_select_fusion), calls=%async_computation.4 | async-start | bytes 3145728 | tf_op jit(solution)/shard_map/all_to_all | solution.py:489
  262.3 79.4 %all-reduce.5.cloned.1.call-start = ((), (), s32[]{:S(2)}) async-start(), calls=%async_computation.13 | async-start | bytes 6291456 | tf_op jit(solution)/shard_map/psum | solution.py:313
  272.0 75.7 %all-gather.4.cloned.1.call-start = ((), (), s32[]{:S(2)}) async-start(), calls=%async_computation.14 | async-start | bytes 1327104 | tf_op jit(solution)/shard_map/all_gather | solution.py:429
  273.8 219.8 %all-reduce.7.cloned.1.call-start = ((), (), s32[]{:S(2)}) async-start(), calls=%async_computation.16 | async-start | bytes 6291456 | tf_op jit(solution)/shard_map/psum | solution.py:291
  297.9 199.7 %copy-start.48 = (f32[1024]{0:T(1024)}, f32[1024]{0:T(1024)S(1)}, u32[]{:S(2)}) copy-start(f32[1024]{0:T(1024)S(1)} %add_divide_fusion) | copy-start | bytes 12292
  425.1 72.4 %copy-start.15 = (bf16[1024,768]{1,0:T(8,128)(2,1)S(1)}, bf16[1024,768]{1,0:T(8,128)(2,1)}, u32[]{:S(2)}) copy-start(bf16[1024,768]{1,0:T(8,128)(2,1)} %gather_fusion.6) | copy-start | bytes 4718596
  515.9 17.0 %all-to-all-start.5 = ((bf16[128,8,192]{0,2,1:T(8,128)(2,1)}), bf16[128,8,192]{0,2,1:T(8,128)(2,1)S(1)}, u32[]{:S(2)}, u32[]{:S(2)}) async-start(bf16[128,8,192]{0,2,1:T(8,128)(2,1)} %copy.140), calls=%async_computation.5 | async-start | bytes 786432 | tf_op jit(solution)/shard_map/all_to_all | solution.py:506
  573.0 30.2 %all-to-all-start.6 = ((bf16[3,128,8,192]{1,3,0,2:T(8,128)(2,1)}), bf16[3,128,8,192]{1,3,0,2:T(8,128)(2,1)}, u32[]{:S(2)}, u32[]{:S(2)}) async-start(bf16[3,128,8,192]{1,3,0,2:T(8,128)(2,1)} %copy.147), calls=%async_computation.6 | async-start | bytes 2359296 | tf_op jit(solution)/shard_map/all_to_all | solution.py:514
  577.3 125.7 %all-reduce.9.cloned.1.call-start = ((), (), s32[]{:S(2)}) async-start(), calls=%async_computation.22 | async-start | bytes 6291456 | tf_op jit(solution)/shard_map/psum | solution.py:259
  635.9 140.4 %reduce-scatter.16.cloned.1.call-start = ((), (), s32[]{:S(2)}) async-start(), calls=%async_computation.20 | async-start | bytes 884736
  638.5 160.2 %reduce-scatter.14.cloned.1.call-start = ((), (), s32[]{:S(2)}) async-start(), calls=%async_computation.19 | async-start | bytes 2654208 | tf_op jit(solution)/shard_map/reduce_scatter | solution.py:544
  642.0 61.0 %copy-start.6 = (bf16[1024,768]{1,0:T(8,128)(2,1)S(1)}, bf16[1024,768]{1,0:T(8,128)(2,1)}, u32[]{:S(2)}) copy-start(bf16[1024,768]{1,0:T(8,128)(2,1)} %gather_fusion.1) | copy-start | bytes 4718596
  642.0 61.0 %copy-start.45 = (f32[1024]{0:T(1024)S(1)}, f32[1024]{0:T(1024)}, u32[]{:S(2)}) copy-start(f32[1024]{0:T(1024)} %copy-done.44) | copy-start | bytes 12292
  642.0 237.0 %reduce-scatter.12.cloned.1.call-start = ((), (), s32[]{:S(2)}) async-start(), calls=%async_computation.18 | async-start | bytes 2654208 | tf_op jit(solution)/shard_map/reduce_scatter | solution.py:543
  717.9 50.6 %all-to-all-start.7 = ((bf16[128,8,768]{2,0,1:T(8,128)(2,1)}), bf16[128,8,768]{2,0,1:T(8,128)(2,1)}, u32[]{:S(2)}, u32[]{:S(2)}) async-start(bf16[128,8,768]{2,0,1:T(8,128)(2,1)} %copy.152), calls=%async_computation.7 | async-start | bytes 3145728 | tf_op jit(solution)/shard_map/all_to_all | solution.py:528
  723.6 219.4 %reduce-scatter.18.cloned.1.call-start = ((), (), s32[]{:S(2)}) async-start(), calls=%async_computation.21 | async-start | bytes 442368
  725.4 289.5 %reduce-scatter.10.cloned.1.call-start = ((), (), s32[]{:S(2)}) async-start(), calls=%async_computation.17 | async-start | bytes 2654208 | tf_op jit(solution)/shard_map/reduce_scatter | solution.py:541
  768.5 265.4 %all-to-all-start.3 = ((bf16[128,8,768]{2,0,1:T(8,128)(2,1)}), bf16[128,8,768]{2,0,1:T(8,128)(2,1)}, u32[]{:S(2)}, u32[]{:S(2)}) async-start(bf16[128,8,768]{2,0,1:T(8,128)(2,1)} %copy.133), calls=%async_computation.3 | async-start | bytes 3145728 | tf_op jit(solution)/shard_map/all_to_all | solution.py:479
  776.3 102.7 %copy-start.29 = (f32[96,768]{1,0:T(8,128)S(1)}, f32[96,768]{1,0:T(8,128)}, u32[]{:S(2)}) copy-start(f32[96,768]{1,0:T(8,128)} %param.49) | copy-start | bytes 884740
  776.3 102.7 %copy-start.34 = (f32[96,768]{1,0:T(8,128)S(1)}, f32[96,768]{1,0:T(8,128)}, u32[]{:S(2)}) copy-start(f32[96,768]{1,0:T(8,128)} %param.54) | copy-start | bytes 884740
  776.3 102.7 %copy-start.35 = (f32[96,768]{1,0:T(8,128)S(1)}, f32[96,768]{1,0:T(8,128)}, u32[]{:S(2)}) copy-start(f32[96,768]{1,0:T(8,128)} %param.59) | copy-start | bytes 884740
  779.1 164.8 %copy-start.56 = (f32[3,96]{1,0:T(4,128)S(1)}, f32[3,96]{1,0:T(4,128)}, u32[]{:S(2)}) copy-start(f32[3,96]{1,0:T(4,128)} %param.51) | copy-start | bytes 3460
  779.1 164.8 %copy-start.58 = (f32[3,96]{1,0:T(4,128)S(1)}, f32[3,96]{1,0:T(4,128)}, u32[]{:S(2)}) copy-start(f32[3,96]{1,0:T(4,128)} %param.56) | copy-start | bytes 3460
  779.1 164.8 %copy-start.59 = (f32[3,96]{1,0:T(4,128)S(1)}, f32[3,96]{1,0:T(4,128)}, u32[]{:S(2)}) copy-start(f32[3,96]{1,0:T(4,128)} %param.61) | copy-start | bytes 3460
  779.1 235.8 %copy-start.31 = (f32[3,96,192]{2,1,0:T(8,128)S(1)}, f32[3,96,192]{2,1,0:T(8,128)}, u32[]{:S(2)}) copy-start(f32[3,96,192]{2,1,0:T(8,128)} %param.47) | copy-start | bytes 663556
  779.1 235.8 %copy-start.36 = (f32[3,96,192]{2,1,0:T(8,128)S(1)}, f32[3,96,192]{2,1,0:T(8,128)}, u32[]{:S(2)}) copy-start(f32[3,96,192]{2,1,0:T(8,128)} %param.52) | copy-start | bytes 663556
  779.1 235.8 %copy-start.37 = (f32[3,96,192]{2,1,0:T(8,128)S(1)}, f32[3,96,192]{2,1,0:T(8,128)}, u32[]{:S(2)}) copy-start(f32[3,96,192]{2,1,0:T(8,128)} %param.57) | copy-start | bytes 663556
  (46 other events, 556.4 us)
Sparse Core Ops, SparseCore 0:
  161.0 45.7 all-gather.5
  275.6 42.3 all-gather.3
  640.0 60.8 reduce-scatter.15
  704.7 93.9 reduce-scatter.13
  802.5 76.4 reduce-scatter.11
  882.5 60.4 reduce-scatter.17
  946.9 67.9 reduce-scatter.9
Sparse Core Ops, SparseCore 1:
  272.0 69.6 all-reduce.4
  425.2 68.3 all-reduce.6
  636.0 66.9 all-reduce.8
where the time goes:
time: 1060 us; the launch traced here: 1050 us
  waiting for transfers between devices  500 us (47%)
  local copies, waits for them, and re-layouts  170 us (16%)
  matrix products  139 us (13%)
  blocking collectives  109 us (10%)
  other arithmetic  73.5 us (7%)
  starting transfers between devices  40.2 us (4%)
  between operations  19.2 us (2%)
    reduce_scatter x1, waiting for transfers between devices, local(): lax.psum_scatter(up_grad, 'dp', scatter_dimension=0, tiled=True)  78.1 us
    reduce_scatter x1, waiting for transfers between devices, local(): lax.psum_scatter(qkv_wgrad, 'dp', scatter_dimension=1, tiled=True)  70.4 us
    psum x1, waiting for transfers between devices, feed_back(): normed_grad = lax.psum(input_part, 'mp')  68.4 us
    unnamed x12, waiting for transfers between devices  62.6 us
    psum x1, waiting for transfers between devices, feed_forward(): return lax.psum(partial_rows.astype(jnp.bfloat16), 'mp').astype(jnp.float32)  60.4 us
    dot_general x15, matrix products, contract_rows(): lax.dot_general(left_side, right_side, (((0,), (0,)), ((), ())), preferre...  48.7 us
    psum x1, waiting for transfers between devices, second_rows(): attended = lax.psum(partial_rows, 'mp')  43.8 us
    all_gather x1, blocking collectives, local(): lax.all_gather(qkv_master.astype(low_type), 'dp', axis=1, tiled=True)  40.5 us
  transfers between devices with their start and end apart: 18, of which 12 were waited for; matrix products, arithmetic and copies ran while one was open for 14% of the time, Pallas kernels for 0%

commit v1 on v0

v1 whole, which is shorter than its diff:
```python
import functools

import jax
import jax.numpy as jnp
from jax import lax
from jax.experimental import pallas as pl
from jax.experimental.pallas import tpu as pltpu
from jax.sharding import PartitionSpec as P

HEAD_DIM = 64
STEP = 10
NORM_EPS = 1e-05
MASKED_SCORE = -1000000000.0
MOMENT_DECAY = 0.9
SQUARE_DECAY = 0.95
ADAM_EPS = 1e-08
WEIGHT_DECAY = 0.1
RATE_MATRIX = 0.06
RATE_VECTOR = 0.2

LOW = jnp.bfloat16
FULL = jnp.float32
MESH = pl.DeviceIdType.MESH
BLOCKS = 4
VMEM_BYTES = 58 * 2**20


def nn(a, b):
    return lax.dot_general(a, b, (((1,), (0,)), ((), ())), preferred_element_type=FULL)


def nt(a, b):
    return lax.dot_general(a, b, (((1,), (1,)), ((), ())), preferred_element_type=FULL)


def tn(a, b):
    return lax.dot_general(a, b, (((0,), (0,)), ((), ())), preferred_element_type=FULL)


def mean_square_inverse(values):
    return lax.rsqrt(jnp.mean(values * values, axis=-1, keepdims=True) + NORM_EPS)


def gate_of(rows, router_row):
    width = rows.shape[-1]
    logit = jnp.sum(rows * router_row, axis=-1, keepdims=True) * width ** (-0.5)
    return jax.nn.sigmoid(logit)


def greet(partners):
    barrier = pltpu.get_barrier_semaphore()
    for partner in partners:
        pl.semaphore_signal(barrier, inc=1, device_id=partner, device_id_type=MESH)
    pl.semaphore_wait(barrier, len(partners))


def remote(src, dst, send_sem, recv_sem, device):
    return pltpu.make_async_remote_copy(
        src_ref=src,
        dst_ref=dst,
        send_sem=send_sem,
        recv_sem=recv_sem,
        device_id=device,
        device_id_type=MESH,
    )


def places(groups):
    me = lax.axis_index("dp")
    part = lax.axis_index("mp")
    line = groups // 2
    return me, part, line, me // 2, me % 2


class Exchange:
    def __init__(self, parts, near, pair, far, total, sems):
        self.parts, self.near, self.pair, self.far, self.total = parts, near, pair, far, total
        self.sems = sems
        self.me, self.part = lax.axis_index("dp"), lax.axis_index("mp")
        self.half = self.part % 2
        self.near_device = (self.me, self.part + 1 - 2 * self.half)
        self.far_device = (self.me, (self.part + 2) % 4)

    def copy(self, which, block, src, dst):
        device = self.far_device if which == 1 else self.near_device
        return remote(src, dst, self.sems.at[0, which, block], self.sems.at[1, which, block], device)

    def out(self, which, block):
        if which == 0:
            return self.copy(0, block, self.parts.at[block, 1 - self.half], self.near.at[block])
        if which == 1:
            return self.copy(1, block, self.pair.at[block], self.far.at[block])
        spot = self.total.at[block, self.half]
        return self.copy(2, block, spot, spot)

    def into(self, which, block):
        spot = (self.near.at[block], self.far.at[block], self.total.at[block, 1 - self.half])[which]
        return self.copy(which, block, spot, spot)

    def put(self, block, value):
        rows, width = value.shape
        self.parts[block] = value.astype(LOW).reshape(2, rows // 2, width)
        self.send(block)

    def send(self, block):
        self.out(0, block).start()

    def cross(self, block):
        self.into(0, block).wait_recv()
        self.pair[block] = (
            self.parts[block, self.half].astype(FULL) + self.near[block].astype(FULL)
        ).astype(LOW)
        self.out(1, block).start()

    def finish(self, block):
        self.into(1, block).wait_recv()
        self.total[block, self.half] = (
            self.pair[block].astype(FULL) + self.far[block].astype(FULL)
        ).astype(LOW)
        self.out(2, block).start()

    def arrived(self, block):
        self.into(2, block).wait_recv()

    def drain(self, block):
        for which in range(3):
            self.out(which, block).wait_send()


def head_lanes(width, head):
    lanes = lax.broadcasted_iota(jnp.int32, (1, width), 1)
    return (lanes // HEAD_DIM == head).astype(FULL).astype(LOW)


def first_kernel(groups, joined, *refs):
    if joined:
        (count_ref, sel_ref, tok_ref, cot_ref, shard_ref, vec_ref), refs = refs[:6], refs[6:]
        (wg, gains, x_ref, dy_ref, qkv_ref, o_ref), refs = refs[:6], refs[6:]
        vg, mixed, send_z, recv_z, send_y, recv_y, send_f, recv_f = refs
    else:
        (count_ref, sel_ref, tok_ref, cot_ref, wg, gains), refs = refs[:6], refs[6:]
        (x_ref, dy_ref, qkv_ref, o_ref), refs = refs[:4], refs[4:]
        (mixed,) = refs
    slots, width = x_ref.shape
    seq_len = tok_ref.shape[0]
    local_width = o_ref.shape[1]
    heads = local_width // HEAD_DIM
    count = count_ref[0]

    if joined:
        me, part, line, place, side = places(groups)
        other = (me + 1 - 2 * side, part)
        peers = [lax.rem(place + j, line) * 2 + side for j in range(1, line)]
        sources = [lax.rem(place + line - j, line) * 2 + side for j in range(1, line)]
        greet([other] + [(peer, part) for peer in peers])

        def slot(k, d):
            return vg.at[d] if k == 3 else wg.at[k, d]

        def source(k):
            return vec_ref if k == 3 else shard_ref.at[k]

        def to_line(k, j):
            return remote(
                source(k), slot(k, me), send_z.at[k, j], recv_z.at[k, j], (peers[j], part)
            )

        def from_line(k, j):
            spot = slot(k, sources[j])
            return remote(spot, spot, send_z.at[k, j], recv_z.at[k, j], (peers[j], part))

        def to_pair(k):
            return remote(source(k), slot(k, me), send_y.at[k], recv_y.at[k], other)

        def from_pair(k):
            spot = slot(k, me + 1 - 2 * side)
            return remote(spot, spot, send_y.at[k], recv_y.at[k], other)

        def forward(k, j):
            spot = slot(k, sources[j])
            return remote(spot, spot, send_f.at[k, j], recv_f.at[k, j], other)

        def forwarded(k, j):
            spot = slot(k, sources[j] + 1 - 2 * side)
            return remote(spot, spot, send_f.at[k, j], recv_f.at[k, j], other)

        def begin(k):
            for j in range(line - 1):
                to_line(k, j).start()
            to_pair(k).start()

        def relay(k):
            for j in range(line - 1):
                from_line(k, j).wait_recv()
                forward(k, j).start()

        def arrive(k):
            from_pair(k).wait_recv()
            for j in range(line - 1):
                forwarded(k, j).wait_recv()

        def drain(k):
            to_pair(k).wait_send()
            for j in range(line - 1):
                to_line(k, j).wait_send()
                forward(k, j).wait_send()

        begin(3)
        begin(0)
        for k in range(3):
            wg[k, me] = shard_ref[k]
        vg[me] = vec_ref[...]

    block = slots // 2

    def pick(number, table_ref, dead_zero, out_ref):
        rows = pl.ds(pl.multiple_of(number * block, block), block)
        spots = lax.broadcasted_iota(jnp.int32, (block, seq_len), 1)
        hot = (spots == sel_ref[rows, :]).astype(FULL).astype(LOW)
        got = nn(hot, table_ref[...])
        if dead_zero:
            ids = number * block + lax.broadcasted_iota(jnp.int32, (block, 1), 0)
            got = jnp.where(ids < count, got, 0.0)
        out_ref[rows, :] = got.astype(LOW)

    @pl.loop(0, 2)
    def _(number):
        pick(number, tok_ref, False, x_ref)

    if joined:
        relay(3)
        relay(0)
        begin(1)

    @pl.loop(0, 2)
    def _(number):
        pick(number, cot_ref, True, dy_ref)

    if joined:
        arrive(3)
        arrive(0)
        share = width // groups
        rows = [vg[d].astype(FULL)[:, :share] for d in range(groups)]
        gains[...] = jnp.concatenate(rows, axis=1)[: gains.shape[0]]

    first_gain = gains[0:1, :]
    w_first = wg[0].reshape(width, wg.shape[-1])
    quarter = slots // BLOCKS

    for t in range(3):
        w_t = w_first[:, t * local_width : (t + 1) * local_width]
        for number in range(BLOCKS):
            rows = slice(number * quarter, (number + 1) * quarter)
            x_rows = x_ref[rows, :].astype(FULL)
            normed = (x_rows * mean_square_inverse(x_rows) * first_gain).astype(LOW)
            qkv_ref[t, rows, :] = nn(normed, w_t).astype(LOW)

    if joined:
        relay(1)
        begin(2)

    mixed[...] = jnp.zeros_like(mixed)

    @pl.loop(0, heads)
    def _(head):
        lanes = head_lanes(local_width, head)
        for number in range(BLOCKS):
            start, stop = number * quarter, (number + 1) * quarter
            query = qkv_ref[0, start:stop, :] * (lanes * HEAD_DIM ** (-0.5))
            scores = nt(query, qkv_ref[1, :stop, :])
            own = start + lax.broadcasted_iota(jnp.int32, (quarter, 1), 0)
            last = jnp.minimum(own, count - 1)
            keys = lax.broadcasted_iota(jnp.int32, (quarter, stop), 1)
            scores = jnp.where(keys <= last, scores, MASKED_SCORE)
            terms = jnp.exp(scores - jnp.max(scores, axis=-1, keepdims=True))
            inverse = 1.0 / jnp.sum(terms, axis=-1, keepdims=True)
            probs = (terms * inverse).astype(LOW)
            mixed[start:stop, :] += nn(probs, qkv_ref[2, :stop, :] * lanes)

    o_ref[...] = mixed[...].astype(LOW)

    if joined:
        relay(2)
        arrive(1)
        arrive(2)
        for k in range(4):
            drain(k)


def second_kernel(*refs):
    (o_ref, x_ref, dy_ref, w_ref, gains), refs = refs[:5], refs[5:]
    (a_ref, m_ref, dz_ref, do_ref, du_ref, dd_ref, dwo_ref, dg_ref), refs = refs[:8], refs[8:]
    a_parts, a_near, a_pair, a_far, h_parts, h_near, h_pair, h_far, h_total = refs[:9]
    up_acc, down_acc, out_acc, a_sems, h_sems = refs[9:]
    width = x_ref.shape[1]
    local_width = o_ref.shape[1]
    rows_of = x_ref.shape[0] // BLOCKS
    first = Exchange(a_parts, a_near, a_pair, a_far, a_ref, a_sems)
    second = Exchange(h_parts, h_near, h_pair, h_far, h_total, h_sems)
    greet([first.near_device, first.far_device])
    w_out = w_ref[0, :, 3 * local_width : 4 * local_width]
    gain_row, router_row = gains[1:2, :], gains[2:3, :]

    def rows_at(number):
        return pl.ds(pl.multiple_of(number * rows_of, rows_of), rows_of)

    @pl.loop(0, BLOCKS)
    def _(number):
        first.put(number, nt(o_ref[rows_at(number), :], w_out))

    @pl.loop(0, BLOCKS)
    def _(number):
        first.cross(number)

    first.finish(0)
    up_acc[...] = jnp.zeros_like(up_acc)
    down_acc[...] = jnp.zeros_like(down_acc)
    out_acc[...] = jnp.zeros_like(out_acc)
    dg_ref[...] = jnp.zeros_like(dg_ref)

    def summed(number):
        x_rows = x_ref[rows_at(number), :].astype(FULL)
        attended = a_ref[number].reshape(rows_of, width).astype(FULL)
        summed_rows = (x_rows + attended).astype(LOW).astype(FULL)
        inverse = mean_square_inverse(summed_rows)
        return x_rows, summed_rows * inverse, inverse

    @pl.loop(0, BLOCKS)
    def _(number):
        rows = rows_at(number)
        first.arrived(number)
        x_rows, normed, inverse = summed(number)
        inner = (normed * gain_row).astype(LOW)
        up = nn(inner, w_ref[1])
        square = up * up
        bent = jnp.tanh(0.7978845608028654 * (up + 0.044715 * square * up))
        half = 0.5 * (1.0 + bent)
        active = (up * half).astype(LOW)
        slope = half + 0.5 * up * (1.0 - bent * bent) * (
            0.7978845608028654 * (1.0 + 3.0 * 0.044715 * square)
        )
        m_ref[rows, :] = nt(active, w_ref[2]).astype(LOW)

        @pl.when(number < BLOCKS - 1)
        def _():
            first.finish(number + 1)

        @pl.when(number > 0)
        def _():
            second.cross(number - 1)

        gate = gate_of(x_rows, router_row)
        branch = (gate * dy_ref[rows, :].astype(FULL)).astype(LOW)
        up_low = (nn(branch, w_ref[2]) * slope).astype(LOW)
        second.put(number, nt(up_low, w_ref[1]))
        down_acc[...] += tn(branch, active)
        up_acc[...] += tn(inner, up_low)

    second.cross(BLOCKS - 1)
    second.finish(0)
    du_ref[...] = up_acc[...].astype(LOW)
    dd_ref[...] = down_acc[...].astype(LOW)

    @pl.loop(0, BLOCKS)
    def _(number):
        rows = rows_at(number)

        @pl.when(number < BLOCKS - 1)
        def _():
            second.finish(number + 1)

        second.arrived(number)
        x_rows, normed, inverse = summed(number)
        grad = h_total[number].reshape(rows_of, width).astype(FULL)
        dg_ref[0:1, :] += jnp.sum(grad * normed, axis=0, keepdims=True)
        scaled = grad * gain_row
        back = inverse * (scaled - normed * jnp.mean(scaled * normed, axis=-1, keepdims=True))
        back_low = back.astype(LOW)
        dz_ref[rows, :] = back_low
        gate = gate_of(x_rows, router_row)
        attn = (gate * dy_ref[rows, :].astype(FULL) + back_low.astype(FULL)).astype(LOW)
        do_ref[rows, :] = nn(attn, w_out).astype(LOW)
        out_acc[...] += tn(attn, o_ref[rows, :])

    dwo_ref[...] = out_acc[...].astype(LOW)

    @pl.loop(0, BLOCKS)
    def _(number):
        first.drain(number)
        second.drain(number)


def third_kernel(groups, joined, *refs):
    (count_ref, x_ref, dy_ref, a_ref, m_ref, dz_ref, do_ref, qkv_ref, w_ref), refs = refs[:9], refs[9:]
    (du_ref, dd_ref, dwo_ref, dg_ref, gains), refs = refs[:5], refs[5:]
    (y_ref, dx_ref, gsum_ref, vsum_ref), refs = refs[:4], refs[4:]
    m_near, m_pair, m_far, m_total, d_parts, d_near, d_pair, d_far, d_total = refs[:9]
    h_ref, dqkv, dqkv_low, vacc, m_sems, d_sems = refs[9:15]
    refs = refs[15:]
    slots, width = x_ref.shape
    local_width = do_ref.shape[1]
    heads = local_width // HEAD_DIM
    rows_of = slots // BLOCKS
    count = count_ref[0]
    branch = Exchange(m_ref, m_near, m_pair, m_far, m_total, m_sems)
    inputs = Exchange(d_parts, d_near, d_pair, d_far, d_total, d_sems)
    partners = [branch.near_device, branch.far_device]
    if joined:
        g0, ry, pairs, rz, vr, send_y, recv_y, send_z, recv_z, send_v, recv_v = refs
        me, part, line, place, side = places(groups)
        other = (me + 1 - 2 * side, part)
        peers = [lax.rem(place + j, line) for j in range(1, line)]
        everyone = [(lax.rem(me + j, groups), part) for j in range(1, groups)]
        greet(partners + everyone)
        grads = (g0, du_ref, dd_ref)

        def to_pair(k, z):
            spot = z * 2 + 1 - side
            return remote(grads[k].at[spot], ry.at[k, z], send_y.at[k, z], recv_y.at[k, z], other)

        def to_line(k, j):
            return remote(
                pairs.at[k, peers[j]],
                rz.at[k, j],
                send_z.at[k, j],
                recv_z.at[k, j],
                (peers[j] * 2 + side, part),
            )

        def begin(k):
            for z in range(line):
                to_pair(k, z).start()

        def relay(k):
            for z in range(line):
                to_pair(k, z).wait_recv()
                pairs[k, z] = (
                    grads[k][z * 2 + side].astype(FULL) + ry[k, z].astype(FULL)
                ).astype(LOW)
            for j in range(line - 1):
                to_line(k, j).start()

        def arrive(k):
            total = pairs[k, place].astype(FULL)
            for j in range(line - 1):
                to_line(k, j).wait_recv()
                total = total + rz[k, j].astype(FULL)
            gsum_ref[k] = total

        def to_all(j):
            return remote(vacc, vr.at[j], send_v.at[j], recv_v.at[j], everyone[j])

        begin(1)
        begin(2)
    else:
        greet(partners)

    branch.send(0)
    dqkv[...] = jnp.zeros_like(dqkv)

    @pl.loop(0, heads)
    def _(head):
        lanes = head_lanes(local_width, head)
        for number in range(BLOCKS):
            start, stop = number * rows_of, (number + 1) * rows_of
            query = qkv_ref[0, start:stop, :] * (lanes * HEAD_DIM ** (-0.5))
            mixed_grad = do_ref[start:stop, :] * lanes
            scores = nt(qkv_ref[1, :stop, :], query)
            own = start + lax.broadcasted_iota(jnp.int32, (1, rows_of), 1)
            last = jnp.minimum(own, count - 1)
            keys = lax.broadcasted_iota(jnp.int32, (stop, rows_of), 0)
            scores = jnp.where(keys <= last, scores, MASKED_SCORE)
            terms = jnp.exp(scores - jnp.max(scores, axis=0, keepdims=True))
            inverse = 1.0 / jnp.sum(terms, axis=0, keepdims=True)
            probs = terms * inverse
            prob_grad = nt(qkv_ref[2, :stop, :], mixed_grad)
            dots = jnp.sum(prob_grad * probs, axis=0, keepdims=True)
            score_grad = (probs * (prob_grad - dots)).astype(LOW)
            dqkv[2, :stop, :] += nn(probs.astype(LOW), mixed_grad)
            dqkv[1, :stop, :] += nn(score_grad, query)
            dqkv[0, start:stop, :] += tn(score_grad, qkv_ref[1, :stop, :] * lanes)

        @pl.when(head == 0)
        def _():
            branch.cross(0)
            if joined:
                relay(1)

        @pl.when(head == 1)
        def _():
            if joined:
                relay(2)

    dqkv_low[0] = (dqkv[0] * HEAD_DIM ** (-0.5)).astype(LOW)
    dqkv_low[1] = dqkv[1].astype(LOW)
    dqkv_low[2] = dqkv[2].astype(LOW)
    first_gain, router_row = gains[0:1, :], gains[2:3, :]

    for number in range(BLOCKS):
        rows = slice(number * rows_of, (number + 1) * rows_of)
        total = jnp.zeros((rows_of, width), FULL)
        for t in range(3):
            w_t = w_ref[:, t * local_width : (t + 1) * local_width]
            total += nt(dqkv_low[t, rows, :], w_t)
        inputs.put(number, total)

    for number in range(BLOCKS):
        inputs.cross(number)
    branch.finish(0)

    for number in range(BLOCKS):
        rows = slice(number * rows_of, (number + 1) * rows_of)
        x_rows = x_ref[rows, :].astype(FULL)
        h_ref[rows, :] = (x_rows * mean_square_inverse(x_rows) * first_gain).astype(LOW)
    parts = [tn(h_ref[...], dqkv_low[t]) for t in range(3)]
    parts.append(dwo_ref[...].astype(FULL))
    merged = jnp.concatenate(parts, axis=1)
    if joined:
        g0[...] = merged.astype(LOW).reshape(g0.shape)
        begin(0)
    else:
        gsum_ref[0] = merged
        gsum_ref[1] = du_ref[...].astype(FULL)
        gsum_ref[2] = dd_ref[...].astype(FULL)

    vacc[...] = jnp.zeros_like(vacc)
    vacc[1:2, :] = dg_ref[0:1, :]
    branch.arrived(0)
    if joined:
        relay(0)
    inputs.finish(0)

    for number in range(BLOCKS):
        rows = slice(number * rows_of, (number + 1) * rows_of)
        if number + 1 < BLOCKS:
            inputs.finish(number + 1)
        x_rows = x_ref[rows, :].astype(FULL)
        dy_rows = dy_ref[rows, :].astype(FULL)
        half, inner = number // (BLOCKS // 2), number % (BLOCKS // 2)
        m_rows = m_total[0, half, inner * rows_of : (inner + 1) * rows_of, :].astype(FULL)
        added = a_ref[rows, :].astype(FULL) + m_rows
        gate = gate_of(x_rows, router_row)
        y_ref[rows, :] = (x_rows + gate * added).astype(LOW)
        gate_grad = jnp.sum(dy_rows * added, axis=-1, keepdims=True)
        logit_grad = gate_grad * gate * (1.0 - gate) * width ** (-0.5)
        inverse = mean_square_inverse(x_rows)
        normed = x_rows * inverse
        inputs.arrived(number)
        grad = d_total[number].reshape(rows_of, width).astype(FULL)
        vacc[0:1, :] += jnp.sum(grad * normed, axis=0, keepdims=True)
        vacc[2:3, :] += jnp.sum(logit_grad * x_rows, axis=0, keepdims=True)
        scaled = grad * first_gain
        back = inverse * (scaled - normed * jnp.mean(scaled * normed, axis=-1, keepdims=True))
        dx_ref[rows, :] = (
            dy_rows + dz_ref[rows, :].astype(FULL) + back + logit_grad * router_row
        ).astype(LOW)

    if joined:
        for j in range(groups - 1):
            to_all(j).start()
        for k in (1, 2, 0):
            arrive(k)
        total = vacc[...]
        for j in range(groups - 1):
            to_all(j).wait_recv()
            total = total + vr[j]
        vsum_ref[...] = total
        for k in range(3):
            for z in range(line):
                to_pair(k, z).wait_send()
            for j in range(line - 1):
                to_line(k, j).wait_send()
        for j in range(groups - 1):
            to_all(j).wait_send()
    else:
        vsum_ref[...] = vacc[...]

    branch.drain(0)
    for number in range(BLOCKS):
        inputs.drain(number)


def place_kernel(count_ref, sel_ref, tok_ref, cot_ref, y_ref, dx_ref, out_ref, grad_ref):
    rows, width = tok_ref.shape
    slots = y_ref.shape[0]
    spots = pl.program_id(0) * rows + lax.broadcasted_iota(jnp.int32, (rows, slots), 0)
    ids = lax.broadcasted_iota(jnp.int32, (1, slots), 1)
    chosen = jnp.where(ids < count_ref[0], sel_ref[...], -1)
    hot = (spots == chosen).astype(FULL)
    hit = jnp.max(hot, axis=-1, keepdims=True) > 0.5
    hot = hot.astype(LOW)
    out_ref[...] = jnp.where(hit, nn(hot, y_ref[...]), tok_ref[...].astype(FULL)).astype(LOW)
    grad_ref[...] = jnp.where(hit, nn(hot, dx_ref[...]), cot_ref[...].astype(FULL))


def adam_update(master, first_moment, second_moment, gradient, step_rate, decay_rate):
    first_new = MOMENT_DECAY * first_moment + (1.0 - MOMENT_DECAY) * gradient
    second_new = SQUARE_DECAY * second_moment + (1.0 - SQUARE_DECAY) * gradient * gradient
    first_hat = first_new / (1.0 - MOMENT_DECAY**STEP)
    second_hat = second_new / (1.0 - SQUARE_DECAY**STEP)
    master_new = master - step_rate * (
        first_hat / (jnp.sqrt(second_hat) + ADAM_EPS) + decay_rate * master
    )
    return (master_new, first_new, second_new)


def shape(dims, kind):
    return jax.ShapeDtypeStruct(dims, kind)


IN_VMEM = pl.BlockSpec(memory_space=pltpu.VMEM)
IN_SMEM = pl.BlockSpec(memory_space=pltpu.SMEM)
DMA = pltpu.SemaphoreType.DMA


def params(number=None):
    if number is None:
        return pltpu.CompilerParams(vmem_limit_bytes=VMEM_BYTES)
    return pltpu.CompilerParams(
        vmem_limit_bytes=VMEM_BYTES, collective_id=number, has_side_effects=True
    )


def local(
    tokens,
    cotangent,
    capacity,
    selected,
    qkv_master,
    out_master,
    up_master,
    down_master,
    vec_master,
    qkv_first,
    out_first,
    up_first,
    down_first,
    vec_first,
    qkv_second,
    out_second,
    up_second,
    down_second,
    vec_second,
):
    groups = lax.axis_size("dp")
    me = lax.axis_index("dp")
    share, local_width = qkv_master.shape[1:]
    hidden = up_master.shape[1]
    width = tokens.shape[2]
    seq_len = tokens.shape[1]
    slots = selected.shape[1]
    joined = share % 16 == 0 and groups % 2 == 0
    count = lax.dynamic_slice_in_dim(capacity, me, 1)
    sel_column = selected.reshape(slots, 1)
    token_rows, cot_rows = tokens[0], cotangent[0]
    line = groups // 2

    first_shard = jnp.concatenate(
        [qkv_master[0], qkv_master[1], qkv_master[2], out_master.T], axis=1
    )
    shard = jnp.stack([first_shard, up_master, down_master.T]).astype(LOW)

    row_outs = [
        shape((slots, width), LOW),
        shape((slots, width), LOW),
        shape((3, slots, local_width), LOW),
        shape((slots, local_width), LOW),
    ]
    if joined:
        vec_pad = jnp.pad(vec_master.astype(LOW), ((0, 13), (0, 128 - share)))
        w_all, gains, x_rows, dy_rows, qkv_rows, mixed = pl.pallas_call(
            functools.partial(first_kernel, groups, True),
            out_shape=[
                shape((3, groups, share, width), LOW),
                shape((8, width), FULL),
            ]
            + row_outs,
            in_specs=[IN_SMEM] + [IN_VMEM] * 5,
            out_specs=[IN_VMEM] * 6,
            scratch_shapes=[
                pltpu.VMEM((groups, 16, 128), LOW),
                pltpu.VMEM((slots, local_width), FULL),
                DMA((4, line - 1)),
                DMA((4, line - 1)),
                DMA((4,)),
                DMA((4,)),
                DMA((4, line - 1)),
                DMA((4, line - 1)),
            ],
            compiler_params=params(0),
            name="first",
        )(count, sel_column, token_rows, cot_rows, shard, vec_pad)
        w_all = w_all.reshape(3, width, width)
    else:
        w_all = lax.all_gather(shard, "dp", axis=1, tiled=True)
        gains = lax.all_gather(vec_master.astype(LOW), "dp", axis=1, tiled=True)
        gains = jnp.pad(gains.astype(FULL), ((0, 5), (0, 0)))
        x_rows, dy_rows, qkv_rows, mixed = pl.pallas_call(
            functools.partial(first_kernel, groups, False),
            out_shape=row_outs,
            in_specs=[IN_SMEM] + [IN_VMEM] * 5,
            out_specs=[IN_VMEM] * 4,
            scratch_shapes=[pltpu.VMEM((slots, local_width), FULL)],
            compiler_params=params(),
            name="first",
        )(count, sel_column, token_rows, cot_rows, w_all, gains)

    quarter = slots // BLOCKS
    half_block = (BLOCKS, quarter // 2, width)
    both_halves = (BLOCKS, 2, quarter // 2, width)
    attended, m_part, dz_rows, mixed_grad, du, dd, dwo, dgain = pl.pallas_call(
        second_kernel,
        out_shape=[
            shape(both_halves, LOW),
            shape((slots, width), LOW),
            shape((slots, width), LOW),
            shape((slots, local_width), LOW),
            shape((width, hidden), LOW),
            shape((width, hidden), LOW),
            shape((width, local_width), LOW),
            shape((8, width), FULL),
        ],
        in_specs=[IN_VMEM] * 5,
        out_specs=[IN_VMEM] * 8,
        scratch_shapes=[
            pltpu.VMEM(both_halves, LOW),
            pltpu.VMEM(half_block, LOW),
            pltpu.VMEM(half_block, LOW),
            pltpu.VMEM(half_block, LOW),
            pltpu.VMEM(both_halves, LOW),
            pltpu.VMEM(half_block, LOW),
            pltpu.VMEM(half_block, LOW),
            pltpu.VMEM(half_block, LOW),
            pltpu.VMEM(both_halves, LOW),
            pltpu.VMEM((width, hidden), FULL),
            pltpu.VMEM((width, hidden), FULL),
            pltpu.VMEM((width, local_width), FULL),
            DMA((2, 3, BLOCKS)),
            DMA((2, 3, BLOCKS)),
        ],
        compiler_params=params(1),
        name="second",
    )(mixed, x_rows, dy_rows, w_all, gains)

    whole_half = (1, slots // 2, width)
    whole_both = (1, 2, slots // 2, width)
    if joined:
        du, dd = (g.reshape(groups, share, hidden) for g in (du, dd))
        grad_out = shape((3, share, width), FULL)
        more_scratch = [
            pltpu.VMEM((groups, share, width), LOW),
            pltpu.VMEM((3, line, share, width), LOW),
            pltpu.VMEM((3, line, share, width), LOW),
            pltpu.VMEM((3, line - 1, share, width), LOW),
            pltpu.VMEM((groups - 1, 8, width), FULL),
            DMA((3, line)),
            DMA((3, line)),
            DMA((3, line - 1)),
            DMA((3, line - 1)),
            DMA((groups - 1,)),
            DMA((groups - 1,)),
        ]
    else:
        grad_out = shape((3, width, width), FULL)
        more_scratch = []
    y_rows, dx_rows, grad_sum, vec_sum = pl.pallas_call(
        functools.partial(third_kernel, groups, joined),
        out_shape=[
            shape((slots, width), LOW),
            shape((slots, width), LOW),
            grad_out,
            shape((8, width), FULL),
        ],
        in_specs=[IN_SMEM] + [IN_VMEM] * 13,
        out_specs=[IN_VMEM] * 4,
        scratch_shapes=[
            pltpu.VMEM(whole_half, LOW),
            pltpu.VMEM(whole_half, LOW),
            pltpu.VMEM(whole_half, LOW),
            pltpu.VMEM(whole_both, LOW),
            pltpu.VMEM(both_halves, LOW),
            pltpu.VMEM(half_block, LOW),
            pltpu.VMEM(half_block, LOW),
            pltpu.VMEM(half_block, LOW),
            pltpu.VMEM(both_halves, LOW),
            pltpu.VMEM((slots, width), LOW),
            pltpu.VMEM((3, slots, local_width), FULL),
            pltpu.VMEM((3, slots, local_width), LOW),
            pltpu.VMEM((8, width), FULL),
            DMA((2, 3, 1)),
            DMA((2, 3, BLOCKS)),
        ]
        + more_scratch,
        compiler_params=params(2),
        name="third",
    )(
        count,
        x_rows,
        dy_rows,
        attended.reshape(slots, width),
        m_part.reshape(whole_both),
        dz_rows,
        mixed_grad,
        qkv_rows,
        w_all[0],
        du,
        dd,
        dwo,
        dgain,
        gains,
    )

    spot_rows = min(256, seq_len)
    by_spot = pl.BlockSpec((spot_rows, width), lambda i: (i, 0))
    block_out, input_grad = pl.pallas_call(
        place_kernel,
        grid=(seq_len // spot_rows,),
        out_shape=[shape((seq_len, width), LOW), shape((seq_len, width), FULL)],
        in_specs=[
            IN_SMEM,
            pl.BlockSpec((1, slots), lambda i: (0, 0)),
            by_spot,
            by_spot,
            pl.BlockSpec((slots, width), lambda i: (0, 0)),
            pl.BlockSpec((slots, width), lambda i: (0, 0)),
        ],
        out_specs=[by_spot, by_spot],
        compiler_params=params(),
        name="place",
    )(count, selected, token_rows, cot_rows, y_rows, dx_rows)

    if joined:
        vec_grad = lax.dynamic_slice_in_dim(vec_sum[:3], me * share, share, 1)
    else:
        grad_sum = lax.psum_scatter(grad_sum, "dp", scatter_dimension=1, tiled=True)
        vec_grad = lax.psum_scatter(vec_sum[:3], "dp", scatter_dimension=1, tiled=True)
    first_sum = grad_sum[0]
    qkv_sum = jnp.stack(
        [first_sum[:, t * local_width : (t + 1) * local_width] for t in range(3)]
    )
    out_sum = first_sum[:, 3 * local_width :].T
    qkv_res = adam_update(qkv_master, qkv_first, qkv_second, qkv_sum, RATE_MATRIX, WEIGHT_DECAY)
    out_res = adam_update(out_master, out_first, out_second, out_sum, RATE_MATRIX, WEIGHT_DECAY)
    up_res = adam_update(up_master, up_first, up_second, grad_sum[1], RATE_MATRIX, WEIGHT_DECAY)
    down_res = adam_update(
        down_master, down_first, down_second, grad_sum[2].T, RATE_MATRIX, WEIGHT_DECAY
    )
    vec_res = adam_update(vec_master, vec_first, vec_second, vec_grad, RATE_VECTOR, 0.0)
    results = (qkv_res, out_res, up_res, down_res, vec_res)
    return (
        block_out[None],
        input_grad[None],
        *(res[0] for res in results),
        *(res[1] for res in results),
        *(res[2] for res in results),
    )


def solution(mesh):
    weights = (
        P(None, "dp", "mp"),
        P("mp", "dp"),
        P("dp", "mp"),
        P("mp", "dp"),
        P(None, "dp"),
    )
    rows = (P("dp", None, None), P("dp", None, None))
    return jax.shard_map(
        local,
        mesh=mesh,
        in_specs=(*rows, P(), P("dp", None), *weights * 3),
        out_specs=(*rows, *weights * 3),
        check_vma=False,
    )
```

time: 1060 us -> 221 us (0.21)
  waiting for transfers between devices: 500 us -> 0 us
  Pallas kernels: 0 us -> 204 us
  local copies, waits for them, and re-layouts: 170 us -> 9.82 us
  matrix products: 139 us -> 0 us
  blocking collectives: 109 us -> 0 us
  other arithmetic: 73.5 us -> 5.94 us
  starting transfers between devices: 40.2 us -> 0 us
  between operations: 19.2 us -> 0.91 us
    pallas_call x0 -> x4, Pallas kernels: none -> 204 us  [the longest x1 85.5 us: local(): pl.pallas_call(functools.partial(third_kernel, groups, joined), out_shape...]
    psum x3 -> x0, waiting for transfers between devices: 173 us -> none  [the longest x1 68.4 us: feed_back(): normed_grad = lax.psum(input_part, 'mp')]
    reduce_scatter x3 -> x0, waiting for transfers between devices: 168 us -> none  [the longest x1 78.1 us: local(): lax.psum_scatter(up_grad, 'dp', scatter_dimension=0, tiled=True)]
    dot_general x80 -> x0, matrix products: 138 us -> none  [the longest x15 48.7 us: contract_rows(): lax.dot_general(left_side, right_side, (((0,), (0,)), ((), ())), preferre...]
    all_gather x3 -> x0, blocking collectives: 109 us -> none  [the longest x1 40.5 us: local(): lax.all_gather(qkv_master.astype(low_type), 'dp', axis=1, tiled=True)]
    all_to_all x8 -> x0, waiting for transfers between devices: 96.3 us -> none  [the longest x1 34.6 us: local(): lax.all_to_all(rows_grad[restore].reshape(spread, groups, model_width).as...]
    unnamed x12 -> x0, waiting for transfers between devices: 62.6 us -> none
    gather x11 -> x0, local copies, waits for them, and re-layouts: 60.6 us -> none  [the longest x1 10.2 us: local(): lax.all_to_all(proj_grad_home.reshape(3, spread, groups, local_width), 'd...]
  transfers between devices with their start and end apart: 18 -> 0, of which waited for: 12 -> 0; matrix products, arithmetic and copies ran while one was open for 14% -> 0% of each run, Pallas kernels for 0% -> 0%
where the time goes in v1:
time: 221 us
  Pallas kernels  204 us (92%)
  local copies, waits for them, and re-layouts  9.82 us (4%)
  other arithmetic  5.94 us (3%)
    pallas_call x1, Pallas kernels, local(): pl.pallas_call(functools.partial(third_kernel, groups, joined), out_shape...  85.5 us
    pallas_call x1, Pallas kernels, local(): pl.pallas_call(functools.partial(first_kernel, groups, True), out_shape=[...  58.2 us
    pallas_call x1, Pallas kernels, local(): pl.pallas_call(second_kernel, out_shape=[shape(both_halves, LOW), shape((...  47.3 us
    pallas_call x1, Pallas kernels, local(): pl.pallas_call(place_kernel, grid=(seq_len // spot_rows,), out_shape=[sha...  13.4 us

profile of v1, /device:TPU:0, one launch (start us, length us, event | category | flops | bytes accessed | tf_op | source)
XLA Modules:
  0.0 221.0 jit_solution(12631296194522055939)
XLA Ops:
  0.7 0.0 copy-start.1
  0.7 0.0 copy-start.2
  0.7 1.3 dynamic_slice.6.refs_0_.count_ref
  2.0 1.0 convert.26
  3.0 0.0 copy-start.13
  3.0 1.0 copy.44
  4.0 0.1 maximum_bitcast_fusion
  4.2 0.8 pad_maximum_fusion.refs_4_
  5.0 1.0 copy.45.refs_1_
  6.0 0.6 pad.4.refs_5_
  6.6 58.2 %first.1 = (bf16[3,8,96,768]{3,2,1,0:T(8,128)(2,1)}, f32[8,768]{1,0:T(8,128)}, bf16[1024,768]{1,0:T(8,128)(2,1)}, bf16[1024,768]{1,0:T(8,128)(2,1)}, bf16[3,1024...) custom-call(s32[1]{0:T(128)} %dynamic_slice.6.refs_0_.count_ref, s32[1024,1]{1,0:T(8,128)} %copy.45.refs_1_, ...), custom_call_target="tpu_custom_call" | custom-call | tf_op jit(solution)/shard_map/first/pallas_call | solution.py:671
  64.8 47.3 %second.1 = (bf16[4,2,128,768]{3,2,1,0:T(8,128)(2,1)}, bf16[1024,768]{1,0:T(8,128)(2,1)}, bf16[1024,768]{1,0:T(8,128)(2,1)}, bf16[1024,192]{1,0:T(8,128)(2,1)}, ...) custom-call(bf16[1024,192]{1,0:T(8,128)(2,1)} %get-tuple-element.39.refs_0_, ...), custom_call_target="tpu_custom_call" | custom-call | tf_op jit(solution)/shard_map/second/pallas_call | solution.py:711
  112.1 2.4 %slice.43 = bf16[1,8,96,768]{3,2,1,0:T(8,128)(2,1)} slice(bf16[3,8,96,768]{3,2,1,0:T(8,128)(2,1)} %get-tuple-element.40), slice={[0:1], [0:8], [0:96], [0:768]} | slice | bytes 2359296 | tf_op jit(solution)/shard_map/slice | solution.py:805
  114.5 85.5 %third.1 = (bf16[1024,768]{1,0:T(8,128)(2,1)}, bf16[1024,768]{1,0:T(8,128)(2,1)}, f32[3,96,768]{2,1,0:T(8,128)}, f32[8,768]{1,0:T(8,128)}) custom-call(s32[1]{0:T(128)} %dynamic_slice.6.refs_0_.count_ref, bf16[1024,768]{1,0:T(8,128)(2,1)} %get-tuple-element.37.refs_1_, bf16[1024,768]{1,0:T(8,128)(2,1)} %get-tuple-element.38.refs_2_, ...), custom_call_target="tpu_custom_call" | custom-call | tf_op jit(solution)/shard_map/third/pallas_call | solution.py:766
  200.0 1.0 slice_bitcast_fusion
  201.0 0.1 slice_bitcast_fusion.4
  201.1 1.1 multiply_subtract_fusion.2
  202.1 13.4 %place.1 = (bf16[2048,768]{1,0:T(8,128)(2,1)}, f32[2048,768]{1,0:T(8,128)}) custom-call(s32[1]{0:T(128)} %dynamic_slice.6.refs_0_.count_ref, s32[1,1024]{1,0:T(1,128)} %sel_ref.1, bf16[2048,768]{1,0:T(8,128)(2,1)} %bitcast.60, bf16[2048,768]{1,0:T(8,128)(2,1)} %bitcast.62, bf16[1024,768]{1,0:T(8,128)(2,1)} %get-tuple-element.51.y_ref, ...), custom_call_target="tpu_custom_call" | custom-call | tf_op jit(solution)/shard_map/place/pallas_call | solution.py:815
  215.5 0.0 copy-start.7
  215.5 0.1 copy.46
  215.7 0.1 copy.47
  215.7 0.0 copy-start.8
  215.8 0.0 copy-start.9
  215.8 0.2 multiply_subtract_fusion.3
  215.9 0.7 copy.50
  216.7 0.7 copy.51
  217.4 0.7 copy.52
  218.2 0.0 copy-start.15
  218.2 0.0 copy-start.16
  218.2 1.0 multiply_subtract_fusion
  219.2 1.0 multiply_subtract_fusion.1
  220.3 0.7 multiply_subtract_fusion.4
  (32 shorter events, 0.1 us)
Async XLA Ops:
  0.7 3.5 %copy-start.1 = (f32[768,96]{0,1:T(8,128)S(1)}, f32[768,96]{0,1:T(8,128)}, u32[]{:S(2)}) copy-start(f32[768,96]{0,1:T(8,128)} %param.26) | copy-start | bytes 884740
  0.7 3.5 %copy-start.2 = (f32[96,768]{1,0:T(8,128)S(1)}, f32[96,768]{1,0:T(8,128)}, u32[]{:S(2)}) copy-start(f32[96,768]{1,0:T(8,128)} %param.25) | copy-start | bytes 884740
  2.0 3.0 %copy-start.12 = (s32[1,1024]{1,0:T(1,128)S(1)}, s32[1,1024]{1,0:T(1,128)}, u32[]{:S(2)}) copy-start(s32[1,1024]{1,0:T(1,128)} %sel_ref.1) | copy-start | bytes 12292
  3.0 3.1 %copy-start.13 = (f32[3,96]{1,0:T(4,128)S(1)}, f32[3,96]{1,0:T(4,128)}, u32[]{:S(2)}) copy-start(f32[3,96]{1,0:T(4,128)} %param.27) | copy-start | bytes 3460
  114.5 86.6 %copy-start = (f32[3,96,192]{2,1,0:T(8,128)S(1)}, f32[3,96,192]{2,1,0:T(8,128)}, u32[]{:S(2)}) copy-start(f32[3,96,192]{2,1,0:T(8,128)} %param.23) | copy-start | bytes 663556
  114.5 86.6 %copy-start.4 = (f32[3,96,192]{2,1,0:T(8,128)S(1)}, f32[3,96,192]{2,1,0:T(8,128)}, u32[]{:S(2)}) copy-start(f32[3,96,192]{2,1,0:T(8,128)} %param.28) | copy-start | bytes 663556
  114.5 86.6 %copy-start.5 = (f32[3,96,192]{2,1,0:T(8,128)S(1)}, f32[3,96,192]{2,1,0:T(8,128)}, u32[]{:S(2)}) copy-start(f32[3,96,192]{2,1,0:T(8,128)} %param.33) | copy-start | bytes 663556
  202.1 13.4 %copy-start.10 = (f32[192,96]{1,0:T(8,128)S(1)}, f32[192,96]{1,0:T(8,128)}, u32[]{:S(2)}) copy-start(f32[192,96]{1,0:T(8,128)} %param.29) | copy-start | bytes 221188
  202.1 13.5 %copy-start.11 = (f32[192,96]{1,0:T(8,128)S(1)}, f32[192,96]{1,0:T(8,128)}, u32[]{:S(2)}) copy-start(f32[192,96]{1,0:T(8,128)} %param.34) | copy-start | bytes 221188
  215.5 2.6 %copy-start.3 = (f32[3,96,768]{2,1,0:T(8,128)S(1)}, f32[3,96,768]{2,1,0:T(8,128)}, u32[]{:S(2)}) copy-start(f32[3,96,768]{2,1,0:T(8,128)} %get-tuple-element.55) | copy-start | bytes 2654212
  215.5 2.6 %copy-start.6 = (f32[768,96]{0,1:T(8,128)S(1)}, f32[768,96]{0,1:T(8,128)}, u32[]{:S(2)}) copy-start(f32[768,96]{0,1:T(8,128)} %param.31) | copy-start | bytes 884740
  215.5 2.6 %copy-start.7 = (f32[768,96]{0,1:T(8,128)S(1)}, f32[768,96]{0,1:T(8,128)}, u32[]{:S(2)}) copy-start(f32[768,96]{0,1:T(8,128)} %param.36) | copy-start | bytes 884740
  215.7 3.5 %copy-start.8 = (f32[96,768]{1,0:T(8,128)S(1)}, f32[96,768]{1,0:T(8,128)}, u32[]{:S(2)}) copy-start(f32[96,768]{1,0:T(8,128)} %param.30) | copy-start | bytes 884740
  215.8 3.5 %copy-start.9 = (f32[96,768]{1,0:T(8,128)S(1)}, f32[96,768]{1,0:T(8,128)}, u32[]{:S(2)}) copy-start(f32[96,768]{1,0:T(8,128)} %param.35) | copy-start | bytes 884740
  218.2 2.1 copy-start.14
  218.2 2.1 copy-start.15
  218.2 2.1 copy-start.16
